TPU v7x, 32 devices: a whole 2x2x4 slice. The times are simulated.
32 devices in a mesh: row: 16 (over z, y, x), col: 2 (over core).
Axes of the slice: x: 2, y: 2, z: 4, core: 2. Of those that a mesh axis runs over, the one named last changes fastest.
Arguments:
- top_inverse: float32 [2, 1024, 1024], P(None, 'row', 'col'), may hold values from -6 to 6, as said below
- blocks_upper: int32 [2, 2], replicated, may hold values from 0 to 3, as said below
- factor_upper: float32 [2, 2, 512, 4096], P(None, None, 'row', 'col'), may hold values from -0.1875 to 0.1875
- diagonal_upper: float32 [2, 2, 4096, 4096], P(None, None, 'row', 'col'), may hold values from -6 to 6, as said below
- parents_lower: int32 [3], replicated, may hold values from 0 to 1
- blocks_lower: int32 [3, 2], replicated, may hold values from 0 to 15, as said below
- factor_lower: float32 [3, 2, 512, 4096], P(None, None, 'row', 'col'), may hold values from -0.1875 to 0.1875
- diagonal_lower: float32 [3, 2, 4096, 4096], P(None, None, 'row', 'col'), may hold values from -6 to 6, as said below
Outputs:
- coupling_inverse_upper: float32 [2, 2, 4096, 512], P(None, None, 'row')
- block_inverse_upper: float32 [2, 2, 4096, 4096], P(None, None, 'row', 'col')
- coupling_inverse_lower: float32 [3, 2, 4096, 512], P(None, None, 'row')
- block_inverse_lower: float32 [3, 2, 4096, 4096], P(None, None, 'row', 'col')
Inputs may be any that keep to these rules, and one draw needn't show every extreme that they name: `top_inverse`: equal to its own transpose (no conjugation) in both parts. `diagonal_upper`: each matrix equals its own transpose (no conjugation) in both parts. `diagonal_lower`: each matrix equals its own transpose (no conjugation) in both parts. `blocks_upper`: each row names 2 different blocks. `blocks_lower`: each row names 2 different blocks.
All inputs are finite; a program needn't handle non-finite values.
Results may differ from a plain program's by a relative error of at most 0.00011.
Values sent between devices are 32-bit elements; how exact they have to be, the bound alone decides.
A program may use at most 256 MiB of HBM per device.

v0:
```python
import jax
import jax.numpy as jnp
from jax import lax
from jax.sharding import PartitionSpec as P

BS = 256
KB = 16
NB = 2
NTB = 4
UPPER = 2


def from_root(block, axis, source):
    block = jnp.where(lax.axis_index(axis) == source, block, jnp.zeros_like(block))
    return lax.psum(block, axis)


def complex_product(first_side, second_side, pattern):
    pieces_all = jnp.einsum(
        pattern,
        first_side,
        second_side,
        precision=lax.Precision.HIGHEST,
        preferred_element_type=jnp.float32,
    )
    real_part = pieces_all[:, 0, 0] - pieces_all[:, 1, 1]
    imag_part = pieces_all[:, 0, 1] + pieces_all[:, 1, 0]
    return jnp.stack([real_part, imag_part], axis=1)


def pick_blocks(stacked, blocks, blocks_total, rows_within, cols_within):
    batch_size = stacked.shape[0]
    tiled_view = stacked.reshape(
        batch_size, 2, rows_within, blocks_total, cols_within, blocks_total
    )

    def pick_single(matrix, chosen):
        matrix = jnp.take(matrix, chosen, axis=2)
        matrix = jnp.take(matrix, chosen, axis=4)
        return matrix.reshape(2, rows_within * NB, cols_within * NB)

    return jax.vmap(pick_single)(tiled_view, blocks)


def supernode_level(chosen, factor_rows, diag_block, slice_start, root_col):
    gathered_factor = lax.all_gather(factor_rows, "row", axis=2, tiled=True)
    factor_columns = lax.dynamic_slice_in_dim(gathered_factor, slice_start, diag_block.shape[2], 3)
    factor_slice = from_root(factor_columns, "col", root_col)
    zeroes = jnp.zeros(
        factor_slice.shape[:2] + (factor_slice.shape[3], chosen.shape[3]), jnp.float32
    )
    factor_part = factor_slice
    coupled_part = zeroes - complex_product(
        factor_part, lax.all_gather(chosen, "row", axis=2, tiled=True), "bikm,bjkn->bijmn"
    )
    incoming = lax.all_gather(coupled_part, "col", axis=3, tiled=True)
    block_total = diag_block
    factor_part = gathered_factor
    block_total = block_total - complex_product(incoming, factor_part, "bimk,bjkn->bijmn")
    gathered = incoming
    block_total, gathered = (block_total, gathered)
    return (gathered, block_total)


def shards(
    top_inverse,
    blocks_upper,
    factor_upper,
    diagonal_upper,
    parents_lower,
    blocks_lower,
    factor_lower,
    diagonal_lower,
):
    row_devices = lax.axis_size("row")
    col_devices = lax.axis_size("col")
    rows_within = BS // row_devices
    cols_within = BS // col_devices
    ratio_axes = row_devices // col_devices
    my_row = lax.axis_index("row")
    root_col = my_row // ratio_axes
    slice_start = my_row % ratio_axes * rows_within * KB
    upper_spans = (0, UPPER)
    first_index, last_index = upper_spans
    width_now = last_index - first_index
    source = jnp.broadcast_to(top_inverse, (width_now,) + top_inverse.shape)
    chosen = pick_blocks(source, blocks_upper, NTB, rows_within, cols_within)
    coupling_out, block_out = supernode_level(
        chosen, factor_upper, diagonal_upper, slice_start, root_col
    )
    upper_coupling = coupling_out
    upper_blocks = block_out
    source = jnp.take(upper_blocks, parents_lower, axis=0)
    chosen = pick_blocks(source, blocks_lower, KB, rows_within, cols_within)
    coupling_out, block_out = supernode_level(
        chosen, factor_lower, diagonal_lower, slice_start, root_col
    )
    return (upper_coupling, upper_blocks, coupling_out, block_out)


def solution(mesh):
    placed = (
        P(None, "row", "col"),
        P(),
        P(None, None, "row", "col"),
        P(None, None, "row", "col"),
        P(),
        P(),
        P(None, None, "row", "col"),
        P(None, None, "row", "col"),
    )
    return jax.shard_map(
        shards,
        mesh=mesh,
        in_specs=placed,
        out_specs=(
            P(None, None, "row", None),
            P(None, None, "row", "col"),
            P(None, None, "row", None),
            P(None, None, "row", "col"),
        ),
        check_vma=False,
    )
```

profile of v0, /device:TPU:0, one launch (start us, length us, event | category | flops | bytes accessed | tf_op | source)
XLA Modules:
  0.0 991.4 jit_solution(4863785366521610066)
XLA Ops:
  8.7 10.8 %broadcast_in_dim.86 = f32[2,16,4,128,4]{4,3,2,1,0:T(8,128)} reshape(f32[2,64,512]{2,1,0:T(8,128)} %param.8) | data formatting | bytes 524288 | tf_op jit(solution)/shard_map/broadcast_in_dim | solution.py:86
  19.5 5.6 copy.76
  26.5 4.6 copy.78
  31.2 7.0 gather.28
  39.1 165.9 %all-gather.9.cloned.1.call-done = f32[2,2,512,2048]{3,2,1,0:T(8,128)} async-done(((f32[2,2,32,2048]{3,2,1,0:T(8,128)}), f32[2,2,512,2048]{3,2,1,0:T(8,128)}) %all-gather.9.cloned.1.call-update) | async-done | bytes 16777232 | tf_op jit(solution)/shard_map/all_gather | solution.py:46
  204.9 3.1 dynamic-slice_select_fusion.1
  208.0 268.8 %all-gather.15.cloned.1.call-done = f32[3,2,512,2048]{3,2,1,0:T(8,128)} async-done(((f32[3,2,32,2048]{3,2,1,0:T(8,128)}), f32[3,2,512,2048]{3,2,1,0:T(8,128)}) %all-gather.15.cloned.1.call-update) | async-done | bytes 25165840 | tf_op jit(solution)/shard_map/all_gather | solution.py:46
  476.8 3.9 dynamic-slice_select_fusion
  480.8 58.5 %all-gather.7.cloned.1.call-done = f32[2,2,512,256]{3,2,1,0:T(8,128)} async-done(((f32[2,2,32,256]{3,2,1,0:T(8,128)}), f32[2,2,512,256]{3,2,1,0:T(8,128)}) %all-gather.7.cloned.1.call-update) | async-done | bytes 2097168 | tf_op jit(solution)/shard_map/all_gather | solution.py:54
  539.2 32.0 %all-reduce.3.cloned.1.call-done = (f32[2,2,512,256]{3,2,1,0:T(8,128)}, f32[3,2,512,256]{3,2,1,0:T(8,128)}) async-done(((f32[2,2,512,256]{3,2,1,0:T(8,128)}, f32[3,2,512,256]{3,2,1,0:T(8,128)}), (f32[2,2,512,256]{3,2,1,0:T(8,128)}, f32[3,2,512,256]{3,2,1,0:T(8,128)})) %all-reduce.3.cloned.1.call-update) | async-done | bytes 5242896 | tf_op jit(solution)/shard_map/psum | solution.py:15
  571.2 5.7 fusion.29
  579.8 10.3 %all-gather.11.cloned.1.call-done = f32[2,2,256,512]{2,3,0,1:T(8,128)} async-done(((f32[2,2,256,256]{2,3,0,1:T(8,128)}), f32[2,2,256,512]{2,3,0,1:T(8,128)}) %all-gather.11.cloned.1.call-update) | async-done | bytes 2097168 | tf_op jit(solution)/shard_map/all_gather | solution.py:56
  590.0 32.2 %fusion.7 = f32[2,2,2,256,2048]{4,3,2,1,0:T(8,128)S(1)} fusion(f32[2,2,512,2048]{3,2,1,0:T(8,128)} %all-gather.9.cloned.1.call-done, f32[2,2,256,512]{2,3,0,1:T(8,128)} %all-gather.11.cloned.1.call-done), kind=kOutput, calls=%fused_computation.15 | convolution fusion | flops 25769803776 | bytes 35651584 | tf_op jit(solution)/shard_map/bimk,bjkn->bijmn/dot_general | solution.py:19
  623.8 4.4 maximum_subtract_fusion.1
  628.3 4.5 fusion.41
  634.0 5.8 gather_fusion.5
  639.9 5.8 gather_fusion.4
  645.6 11.6 %pad_maximum_fusion = f32[3,2,256,2048]{3,2,1,0:T(8,128)} fusion(f32[3,2,256,1024]{3,2,1,0:T(8,128)} %gather_fusion.5, f32[3,2,256,1024]{3,2,1,0:T(8,128)} %gather_fusion.4), kind=kLoop, calls=%fused_computation.11 | loop fusion | flops 3145728 | bytes 25165824
  657.2 53.2 %gather.30 = f32[3,2,16,16,128,16]{5,4,3,2,1,0:T(8,128)} reshape(f32[3,2,256,2048]{3,2,1,0:T(8,128)} %pad_maximum_fusion) | data formatting | bytes 25165824 | tf_op jit(solution)/shard_map/jit(_take)/gather | solution.py:93
  710.4 64.7 %broadcast_select_fusion = f32[3,2,16,16,128,16]{5,4,3,2,1,0:T(8,128)} fusion(f32[3,2,16,16,128,16]{5,4,3,2,1,0:T(8,128)} %gather.30, pred[3]{0:T(512)(128)(4,1)S(1)} %compare_and_fusion), kind=kLoop, calls=%fused_computation.6 | loop fusion | flops 3145728 | bytes 25165828 | tf_op jit(solution)/shard_map/jit(_take)/select_n | solution.py:93
  775.1 11.1 %gather_fusion.2 = f32[6,2,16,128,16]{4,3,2,1,0:T(8,128)} fusion(f32[3,2,16,16,128,16]{5,4,3,2,1,0:T(8,128)} %broadcast_select_fusion, s32[6]{0:T(128)S(1)} %reshape.189), kind=kCustom, calls=%fused_computation.2 | custom fusion | bytes 3145776 | tf_op jit(solution)/shard_map/vmap(jit(_take))/gather | solution.py:38
  786.2 7.6 copy.89
  794.8 6.6 copy.90
  801.4 10.0 %gather.33 = f32[3,2,32,256]{3,2,1,0:T(8,128)S(1)} reshape(f32[3,2,16,2,128,2]{5,4,3,2,1,0:T(8,128)} %copy.90) | data formatting | bytes 393216 | tf_op jit(solution)/shard_map/vmap(jit(_take))/gather | solution.py:39
  812.1 69.7 %all-gather.13.cloned.1.call-done = f32[3,2,512,256]{3,2,1,0:T(8,128)} async-done(((f32[3,2,32,256]{3,2,1,0:T(8,128)}), f32[3,2,512,256]{3,2,1,0:T(8,128)}) %all-gather.13.cloned.1.call-update) | async-done | bytes 3145744 | tf_op jit(solution)/shard_map/all_gather | solution.py:54
  881.8 7.2 fusion.24
  890.6 8.6 copy.98
  901.6 45.8 %fusion.4 = f32[3,2,2,256,2048]{4,3,2,1,0:T(8,128)} fusion(f32[3,2,512,2048]{3,2,1,0:T(8,128)} %all-gather.15.cloned.1.call-done, f32[3,2,256,512]{2,3,0,1:T(8,128)} %all-gather.17.cloned.1.call-done), kind=kOutput, calls=%fused_computation.13 | convolution fusion | flops 38654705664 | bytes 53477376 | tf_op jit(solution)/shard_map/bimk,bjkn->bijmn/dot_general | solution.py:19
  947.5 5.9 fusion.10
  953.4 5.9 fusion.12
  959.3 10.9 %maximum_subtract_fusion = f32[3,2,256,2048]{3,2,0,1:T(8,128)} fusion(f32[3,1,256,2048]{3,2,0,1:T(8,128)S(1)} %fusion.10, f32[3,1,256,2048]{3,2,0,1:T(8,128)S(1)} %fusion.12, f32[3,2,256,2048]{3,2,1,0:T(8,128)} %param.15), kind=kLoop, calls=%fused_computation.12 | loop fusion | flops 6291456 | bytes 37748736 | tf_op jit(solution)/shard_map/sub | solution.py:59
  970.2 11.7 %copy.100 = f32[3,2,256,2048]{3,2,1,0:T(8,128)} copy(f32[3,2,256,2048]{3,2,0,1:T(8,128)} %maximum_subtract_fusion) | data formatting | bytes 25165824
  (64 shorter events, 17.3 us)
Async XLA Ops:
  7.2 197.8 %all-gather.9.cloned.1.call-start = ((), (), s32[]{:S(2)}) async-start(), calls=%async_computation.1 | async-start | bytes 17825792 | tf_op jit(solution)/shard_map/all_gather | solution.py:46
  7.9 468.9 %all-gather.15.cloned.1.call-start = ((), (), s32[]{:S(2)}) async-start(), calls=%async_computation.4 | async-start | bytes 26738688 | tf_op jit(solution)/shard_map/all_gather | solution.py:46
  8.6 530.6 %all-gather.7.cloned.1.call-start = ((), (), s32[]{:S(2)}) async-start(), calls=%async_computation | async-start | bytes 2228224 | tf_op jit(solution)/shard_map/all_gather | solution.py:54
  19.5 5.6 copy-start.5
  39.0 532.2 %all-reduce.3.cloned.1.call-start = ((), (), s32[]{:S(2)}) async-start(), calls=%async_computation.6 | async-start | bytes 10485760 | tf_op jit(solution)/shard_map/psum | solution.py:15
  480.7 109.3 %all-gather.11.cloned.1.call-start = ((), (), s32[]{:S(2)}) async-start(), calls=%async_computation.2 | async-start | bytes 3145728 | tf_op jit(solution)/shard_map/all_gather | solution.py:56
  571.2 7.5 copy-start.6
  571.2 8.6 copy-start.7
  578.2 303.6 %all-gather.13.cloned.1.call-start = ((), (), s32[]{:S(2)}) async-start(), calls=%async_computation.3 | async-start | bytes 3342336 | tf_op jit(solution)/shard_map/all_gather | solution.py:54
  628.3 5.7 copy-start
  801.4 10.0 %copy-start.4 = (pred[3,256]{1,0:T(4,128)(4,1)S(1)}, pred[3,256]{1,0:T(4,128)(4,1)}, u32[]{:S(2)}) copy-start(pred[3,256]{1,0:T(4,128)(4,1)} %broadcast_in_dim.94) | copy-start | bytes 2308
  801.4 80.4 %copy-start.3 = (f32[3,2,512,256]{3,2,1,0:T(8,128)S(1)}, f32[3,2,512,256]{3,2,1,0:T(8,128)}, u32[]{:S(2)}) copy-start(f32[3,2,512,256]{3,2,1,0:T(8,128)} %get-tuple-element.21) | copy-start | bytes 9437188
  812.1 89.6 %all-gather.17.cloned.1.call-start = ((), (), s32[]{:S(2)}) async-start(), calls=%async_computation.5 | async-start | bytes 4718592 | tf_op jit(solution)/shard_map/all_gather | solution.py:56
  890.5 8.6 copy-start.2
  970.2 11.7 %copy-start.1 = (f32[3,2,256,512]{2,3,0,1:T(8,128)S(1)}, f32[3,2,256,512]{2,3,0,1:T(8,128)}, u32[]{:S(2)}) copy-start(f32[3,2,256,512]{2,3,0,1:T(8,128)} %all-gather.17.cloned.1.call-done) | copy-start | bytes 9437188
Sparse Core Ops, SparseCore 0:
  10.8 194.1 all-gather.8
  207.7 269.0 all-gather.14
  480.1 59.0 all-gather.6
  542.2 28.9 all-reduce.2
  578.3 11.7 all-gather.10
  812.2 69.5 all-gather.12
  890.7 10.9 all-gather.16
where the time goes:
time: 999 us; the launch traced here: 991 us
  waiting for transfers between devices  607 us (61%)
  local copies, waits for them, and re-layouts  162 us (16%)
  other arithmetic  116 us (12%)
  matrix products  91.1 us (9%)
  between operations  14.6 us (1%)
    all_gather x2, waiting for transfers between devices, supernode_level(): gathered_factor = lax.all_gather(factor_rows, 'row', axis=2, tiled=True)  435 us
    all_gather x2, waiting for transfers between devices, supernode_level(): lax.all_gather(chosen, 'row', axis=2, tiled=True)  128 us
    dot_general x4, matrix products, complex_product(): jnp.einsum(pattern, first_side, second_side, precision=lax.Precision.HIGH...  91.1 us
    gather x4, local copies, waits for them, and re-layouts, shards(): source = jnp.take(upper_blocks, parents_lower, axis=0)  69.4 us
    select_n x2, other arithmetic, shards(): source = jnp.take(upper_blocks, parents_lower, axis=0)  64.7 us
    psum x1, waiting for transfers between devices, from_root(): return lax.psum(block, axis)  32 us
    gather x6, local copies, waits for them, and re-layouts, pick_single(): matrix = jnp.take(matrix, chosen, axis=4)  29.3 us
    unnamed x20, local copies, waits for them, and re-layouts  25.9 us
  transfers between devices with their start and end apart: 7, of which 7 were waited for; matrix products, arithmetic and copies ran while one was open for 5% of the time, Pallas kernels for 0%

commit v1 on v0

--- a/solution.py
+++ b/solution.py
@@ -10,9 +10,15 @@
 UPPER = 2
 
 
+def gather_and_add(x, name):
+    parts = lax.all_gather(x, name, axis=0, tiled=False)
+    total = parts.sum(axis=0)
+    return total
+
+
 def from_root(block, axis, source):
     block = jnp.where(lax.axis_index(axis) == source, block, jnp.zeros_like(block))
-    return lax.psum(block, axis)
+    return gather_and_add(block, axis)
 
 
 def complex_product(first_side, second_side, pattern):

time: 999 us -> 881 us (0.88)
  waiting for transfers between devices: 607 us -> 480 us
  other arithmetic: 116 us -> 126 us
    all_gather x2, waiting for transfers between devices: 435 us -> 350 us  [supernode_level(): gathered_factor = lax.all_gather(factor_rows, 'row', axis=2, tiled=True)]
    psum x1 -> x0, waiting for transfers between devices: 32 us -> none  [from_root(): return lax.psum(block, axis)]
  transfers between devices with their start and end apart: 7 -> 8, of which waited for: 7 -> 6; matrix products, arithmetic and copies ran while one was open for 5% -> 31% of each run, Pallas kernels for 0% -> 0%
where the time goes in v1:
time: 881 us; the launch traced here: 872 us
  waiting for transfers between devices  480 us (54%)
  local copies, waits for them, and re-layouts  160 us (18%)
  other arithmetic  126 us (14%)
  matrix products  90.4 us (10%)
  between operations  14.9 us (2%)
    all_gather x2, waiting for transfers between devices, supernode_level(): gathered_factor = lax.all_gather(factor_rows, 'row', axis=2, tiled=True)  350 us
    all_gather x2, waiting for transfers between devices, supernode_level(): lax.all_gather(chosen, 'row', axis=2, tiled=True)  121 us
    dot_general x4, matrix products, complex_product(): jnp.einsum(pattern, first_side, second_side, precision=lax.Precision.HIGH...  90.4 us
    gather x4, local copies, waits for them, and re-layouts, shards(): source = jnp.take(upper_blocks, parents_lower, axis=0)  69.4 us
    select_n x2, other arithmetic, shards(): source = jnp.take(upper_blocks, parents_lower, axis=0)  66.4 us
    gather x6, local copies, waits for them, and re-layouts, pick_single(): matrix = jnp.take(matrix, chosen, axis=4)  29.1 us
    unnamed x20, local copies, waits for them, and re-layouts  26 us
    gather x6, local copies, waits for them, and re-layouts, pick_single(): matrix = jnp.take(matrix, chosen, axis=2)  19.5 us
  transfers between devices with their start and end apart: 8, of which 6 were waited for; matrix products, arithmetic and copies ran while one was open for 31% of the time, Pallas kernels for 0%

profile of v1, /device:TPU:0, one launch (start us, length us, event | category | flops | bytes accessed | tf_op | source)
XLA Modules:
  0.0 872.3 jit_solution(3422598973099315887)
XLA Ops:
  8.0 197.0 %all-gather.13.cloned.1.call-done = f32[2,2,512,2048]{3,2,1,0:T(8,128)} async-done(((f32[2,2,32,2048]{3,2,1,0:T(8,128)}), f32[2,2,512,2048]{3,2,1,0:T(8,128)}) %all-gather.13.cloned.1.call-update) | async-done | bytes 16777232 | tf_op jit(solution)/shard_map/all_gather | solution.py:52
  205.0 3.1 dynamic-slice_select_fusion.1
  208.2 10.0 %broadcast_in_dim.86 = f32[2,16,4,128,4]{4,3,2,1,0:T(8,128)} reshape(f32[2,64,512]{2,1,0:T(8,128)S(1)} %copy-done.3) | data formatting | bytes 524288 | tf_op jit(solution)/shard_map/broadcast_in_dim | solution.py:92
  218.2 5.2 copy.101
  224.7 4.6 copy.103
  229.4 6.9 gather.28
  240.0 57.0 %all-gather.11.cloned.1.call-done = f32[2,2,512,256]{3,2,1,0:T(8,128)} async-done(((f32[2,2,32,256]{3,2,1,0:T(8,128)}), f32[2,2,512,256]{3,2,1,0:T(8,128)}) %all-gather.11.cloned.1.call-update) | async-done | bytes 2097168 | tf_op jit(solution)/shard_map/all_gather | solution.py:60
  297.0 5.1 fusion.29
  305.5 7.3 all-gather.15.cloned.1.call-done
  312.8 32.2 %fusion.7 = f32[2,2,2,256,2048]{4,3,2,1,0:T(8,128)S(1)} fusion(f32[2,2,512,2048]{3,2,1,0:T(8,128)} %all-gather.13.cloned.1.call-done, f32[2,2,256,512]{2,3,0,1:T(8,128)} %all-gather.15.cloned.1.call-done), kind=kOutput, calls=%fused_computation.15 | convolution fusion | flops 25769803776 | bytes 35651584 | tf_op jit(solution)/shard_map/bimk,bjkn->bijmn/dot_general | solution.py:25
  346.6 4.5 maximum_subtract_fusion.1
  351.1 4.5 fusion.41
  356.9 5.8 gather_fusion.4
  362.7 5.8 gather_fusion.5
  368.6 12.8 %pad_maximum_fusion = f32[3,2,256,2048]{3,2,1,0:T(8,128)} fusion(f32[3,2,256,1024]{3,2,1,0:T(8,128)} %gather_fusion.5, f32[3,2,256,1024]{3,2,1,0:T(8,128)} %gather_fusion.4), kind=kLoop, calls=%fused_computation.11 | loop fusion | flops 3145728 | bytes 25165824
  381.3 53.3 %gather.30 = f32[3,2,16,16,128,16]{5,4,3,2,1,0:T(8,128)} reshape(f32[3,2,256,2048]{3,2,1,0:T(8,128)} %pad_maximum_fusion) | data formatting | bytes 25165824 | tf_op jit(solution)/shard_map/jit(_take)/gather | solution.py:99
  434.6 152.9 %all-gather.19.cloned.1.call-done = f32[3,2,512,2048]{3,2,1,0:T(8,128)} async-done(((f32[3,2,32,2048]{3,2,1,0:T(8,128)}), f32[3,2,512,2048]{3,2,1,0:T(8,128)}) %all-gather.19.cloned.1.call-update) | async-done | bytes 25165840 | tf_op jit(solution)/shard_map/all_gather | solution.py:52
  587.5 3.9 dynamic-slice_select_fusion
  591.5 66.4 %broadcast_select_fusion = f32[3,2,16,16,128,16]{5,4,3,2,1,0:T(8,128)} fusion(f32[3,2,16,16,128,16]{5,4,3,2,1,0:T(8,128)} %gather.30, pred[3]{0:T(512)(128)(4,1)S(1)} %compare_and_fusion), kind=kLoop, calls=%fused_computation.6 | loop fusion | flops 3145728 | bytes 25165828 | tf_op jit(solution)/shard_map/jit(_take)/select_n | solution.py:99
  657.9 11.1 %gather_fusion.2 = f32[6,2,16,128,16]{4,3,2,1,0:T(8,128)} fusion(f32[3,2,16,16,128,16]{5,4,3,2,1,0:T(8,128)} %broadcast_select_fusion, s32[6]{0:T(128)S(1)} %reshape.189), kind=kCustom, calls=%fused_computation.2 | custom fusion | bytes 3145776 | tf_op jit(solution)/shard_map/vmap(jit(_take))/gather | solution.py:44
  669.0 7.6 copy.114
  677.5 6.6 copy.115
  684.1 9.8 %gather.33 = f32[3,2,32,256]{3,2,1,0:T(8,128)S(1)} reshape(f32[3,2,16,2,128,2]{5,4,3,2,1,0:T(8,128)} %copy.115) | data formatting | bytes 393216 | tf_op jit(solution)/shard_map/vmap(jit(_take))/gather | solution.py:45
  695.0 3.6 reduce_sum.19
  698.6 64.0 %all-gather.17.cloned.1.call-done = f32[3,2,512,256]{3,2,1,0:T(8,128)} async-done(((f32[3,2,32,256]{3,2,1,0:T(8,128)}), f32[3,2,512,256]{3,2,1,0:T(8,128)}) %all-gather.17.cloned.1.call-update) | async-done | bytes 3145744 | tf_op jit(solution)/shard_map/all_gather | solution.py:60
  762.6 7.2 fusion.24
  771.3 8.6 copy.123
  782.4 45.9 %fusion.4 = f32[3,2,2,256,2048]{4,3,2,1,0:T(8,128)} fusion(f32[3,2,512,2048]{3,2,1,0:T(8,128)} %all-gather.19.cloned.1.call-done, f32[3,2,256,512]{2,3,0,1:T(8,128)} %all-gather.21.cloned.1.call-done), kind=kOutput, calls=%fused_computation.13 | convolution fusion | flops 38654705664 | bytes 53477376 | tf_op jit(solution)/shard_map/bimk,bjkn->bijmn/dot_general | solution.py:25
  828.3 5.9 fusion.10
  834.2 5.9 fusion.12
  840.1 10.9 %maximum_subtract_fusion = f32[3,2,256,2048]{3,2,0,1:T(8,128)} fusion(f32[3,1,256,2048]{3,2,0,1:T(8,128)S(1)} %fusion.10, f32[3,1,256,2048]{3,2,0,1:T(8,128)S(1)} %fusion.12, f32[3,2,256,2048]{3,2,1,0:T(8,128)} %param.15), kind=kLoop, calls=%fused_computation.12 | loop fusion | flops 6291456 | bytes 37748736 | tf_op jit(solution)/shard_map/sub | solution.py:65
  851.0 11.7 %copy.125 = f32[3,2,256,2048]{3,2,1,0:T(8,128)} copy(f32[3,2,256,2048]{3,2,0,1:T(8,128)} %maximum_subtract_fusion) | data formatting | bytes 25165824
  (69 shorter events, 20.2 us)
Async XLA Ops:
  7.2 201.0 %copy-start.5 = (s32[2,2]{1,0:T(2,128)S(1)}, s32[2,2]{1,0:T(2,128)}, u32[]{:S(2)}) copy-start(s32[2,2]{1,0:T(2,128)} %param.9) | copy-start | bytes 52
  7.2 201.1 %copy-start.3 = (f32[2,64,512]{2,1,0:T(8,128)S(1)}, f32[2,64,512]{2,1,0:T(8,128)}, u32[]{:S(2)}) copy-start(f32[2,64,512]{2,1,0:T(8,128)} %param.8) | copy-start | bytes 786436
  7.2 197.8 %all-gather.13.cloned.1.call-start = ((), (), s32[]{:S(2)}) async-start(), calls=%async_computation.1 | async-start | bytes 17825792 | tf_op jit(solution)/shard_map/all_gather | solution.py:52
  7.9 229.3 %all-gather.23.cloned.1.call-start = ((), (), s32[]{:S(2)}) async-start(), calls=%async_computation.6 | async-start | bytes 6291456 | tf_op jit(solution)/shard_map/all_gather | solution.py:14
  208.1 88.9 %all-gather.11.cloned.1.call-start = ((), (), s32[]{:S(2)}) async-start(), calls=%async_computation | async-start | bytes 2228224 | tf_op jit(solution)/shard_map/all_gather | solution.py:60
  237.2 75.7 %all-gather.15.cloned.1.call-start = ((), (), s32[]{:S(2)}) async-start(), calls=%async_computation.2 | async-start | bytes 3145728 | tf_op jit(solution)/shard_map/all_gather | solution.py:62
  240.0 64.4 %copy-start.6 = (s32[3,2]{0,1:T(2,128)S(1)}, s32[3,2]{0,1:T(2,128)}, u32[]{:S(2)}) copy-start(s32[3,2]{0,1:T(2,128)} %param.13) | copy-start | bytes 76
  240.0 65.5 %copy-start.7 = (s32[3]{0:T(128)S(1)}, s32[3]{0:T(128)}, u32[]{:S(2)}) copy-start(s32[3]{0:T(128)} %param.12) | copy-start | bytes 40
  303.3 284.2 %all-gather.19.cloned.1.call-start = ((), (), s32[]{:S(2)}) async-start(), calls=%async_computation.4 | async-start | bytes 26738688 | tf_op jit(solution)/shard_map/all_gather | solution.py:52
  303.9 391.0 %all-gather.25.cloned.1.call-start = ((), (), s32[]{:S(2)}) async-start(), calls=%async_computation.7 | async-start | bytes 9437184 | tf_op jit(solution)/shard_map/all_gather | solution.py:14
  351.1 5.8 copy-start
  591.4 171.1 %all-gather.17.cloned.1.call-start = ((), (), s32[]{:S(2)}) async-start(), calls=%async_computation.3 | async-start | bytes 3342336 | tf_op jit(solution)/shard_map/all_gather | solution.py:60
  684.1 9.8 %copy-start.4 = (pred[3,256]{1,0:T(4,128)(4,1)S(1)}, pred[3,256]{1,0:T(4,128)(4,1)}, u32[]{:S(2)}) copy-start(pred[3,256]{1,0:T(4,128)(4,1)} %broadcast_in_dim.94) | copy-start | bytes 2308
  694.7 87.7 %all-gather.21.cloned.1.call-start = ((), (), s32[]{:S(2)}) async-start(), calls=%async_computation.5 | async-start | bytes 4718592 | tf_op jit(solution)/shard_map/all_gather | solution.py:62
  771.3 8.6 copy-start.2
  851.0 11.7 %copy-start.1 = (f32[3,2,256,512]{2,3,0,1:T(8,128)S(1)}, f32[3,2,256,512]{2,3,0,1:T(8,128)}, u32[]{:S(2)}) copy-start(f32[3,2,256,512]{2,3,0,1:T(8,128)} %all-gather.21.cloned.1.call-done) | copy-start | bytes 9437188
Sparse Core Ops, SparseCore 0:
  10.8 194.1 all-gather.12
  208.2 11.8 all-gather.22
  237.3 59.6 all-gather.10
  303.5 9.3 all-gather.14
  315.4 272.0 all-gather.18
  591.5 14.9 all-gather.24
  694.8 67.7 all-gather.16
  771.4 10.9 all-gather.20
